TPU v7x, 256 devices: a whole 4x4x8 slice. The times are simulated.
256 devices in a mesh: dp: 64 (over y, z, core), mp: 4 (over x).
Axes of the slice: x: 4, y: 4, z: 8, core: 2. Of those that a mesh axis runs over, the one named last changes fastest.
Arguments:
- pixels: bfloat16 [9216, 588], P('dp'), may hold values from -40 to 40
- patch_counts: int32 [192], P('dp'), may hold values from 12 to 48, as said below
- pack_index: int32 [192], P('dp'), may hold values from 0 to 63, as said below
- embed_weight: bfloat16 [588, 4, 1536], P(None, 'mp', 'dp'), may hold values from -1 to 1
- norm_gain: float32 [6144], P('mp'), may hold values from 0.5 to 1.5
- query_weight: bfloat16 [6144, 3072], P('dp', 'mp'), may hold values from -0.078125 to 0.078125
- key_weight: bfloat16 [6144, 3072], P('dp', 'mp'), may hold values from -0.078125 to 0.078125
- query_gain: float32 [128], replicated, may hold values from 0.1 to 1.9
- key_gain: float32 [128], replicated, may hold values from 0.1 to 1.9
- cotangent: bfloat16 [12288, 3072], P('dp', 'mp'), may hold values from -0.0625 to 0.0625
Outputs:
- attended: bfloat16 [12288, 3072], P('dp', 'mp')
- embed_grad: float32 [588, 4, 1536], P(None, 'mp', 'dp')
Inputs may be any that keep to these rules, and one draw needn't show every extreme that they name: `patch_counts`: each draw has 4 images of 48 patches in one pack. `pack_index`: the pack of an image held by loader l is l plus one of 0 to 3, modulo the length of the dp axis; the images of one loader go to different packs.
All inputs are finite; a program needn't handle non-finite values.
Results may differ from a plain program's by a relative error of at most 0.015.
Values may be sent and summed in bfloat16 or wider, within the bound.
No kernel may reach another device: no remote copies, remote signals or barrier semaphores. Data moves between devices by JAX's collectives and lax.ppermute only.
A program may use at most 128 MiB of HBM per device.

v0:
```python
import jax
import jax.numpy as jnp
from jax import lax
from jax.sharding import PartitionSpec as P

D = 6144
HEADS = 24
HD = 128
PATCH = 588
MOST = 48
IMG_LOAD = 3
REACH = 4


EPS = 1e-06


def from_behind(block, axis, distance):
    devices = range(lax.axis_size(axis))
    route = [((i - distance) % len(devices), i) for i in devices]
    return lax.ppermute(block, axis, route)


def head_norm(values, heads_here, head_size):
    shaped = values.reshape(values.shape[0], heads_here, head_size)
    center = jnp.mean(shaped, axis=2, keepdims=True)
    spread = jnp.mean(shaped * shaped, axis=2, keepdims=True) - center * center
    inv_spread = lax.rsqrt(spread + EPS)
    return ((shaped - center) * inv_spread, inv_spread)


def head_back(grad_hat, unit_rows, inv_spread, gain_vec):
    grad_unit = grad_hat * gain_vec
    mean_grad = jnp.mean(grad_unit, axis=2, keepdims=True)
    second = jnp.mean(grad_unit * unit_rows, axis=2, keepdims=True)
    return inv_spread * (grad_unit - mean_grad - unit_rows * second)


def attend(query_hat, key_hat, values, grad_out, segment, live_rows, head_size):
    scores = jnp.einsum(
        "bihd,bjhd->bhij", query_hat, key_hat, preferred_element_type=jnp.float32
    ) * head_size ** (-0.5)
    allowed = (
        (segment[:, :, None] == segment[:, None, :]) & live_rows[:, :, None] & live_rows[:, None, :]
    )
    raised = jnp.where(allowed[:, None], jnp.exp(scores), jnp.zeros_like(scores))
    totals = jnp.sum(raised, axis=3, keepdims=True)
    totals = jnp.where(live_rows[:, None, :, None], totals, jnp.ones_like(totals))
    attn_probs = raised / totals
    attn_low = attn_probs.astype(jnp.bfloat16)
    blended = jnp.einsum("bhij,bjhg->bihg", attn_low, values, preferred_element_type=jnp.float32)
    grad_probs = jnp.einsum("bihg,bjhg->bhij", grad_out, values, preferred_element_type=jnp.float32)
    grad_values = jnp.einsum(
        "bhij,bihg->bjhg", attn_low, grad_out, preferred_element_type=jnp.float32
    )
    grad_scores = attn_probs * (
        grad_probs - jnp.sum(attn_probs * grad_probs, axis=3, keepdims=True)
    )
    grad_low = (grad_scores * head_size ** (-0.5)).astype(jnp.bfloat16)
    grad_query = jnp.einsum(
        "bhij,bjhd->bihd", grad_low, key_hat, preferred_element_type=jnp.float32
    )
    grad_key = jnp.einsum(
        "bhij,bihd->bjhd", grad_low, query_hat, preferred_element_type=jnp.float32
    )
    return (blended, grad_values, grad_query, grad_key)


def per_device(
    pixels,
    patch_counts,
    pack_index,
    embed_weight,
    norm_gain,
    query_weight,
    key_weight,
    query_gain,
    key_gain,
    cotangent,
):
    loaders = lax.axis_size("dp")
    groups = lax.axis_size("mp")
    own_index = lax.axis_index("dp")
    heads_here = HEADS // groups
    features = D // groups
    group_width = D // HEADS
    pack_rows = REACH * MOST
    embed_cols = lax.all_gather(embed_weight, "dp", axis=2, tiled=True).reshape(PATCH, features)
    positions = jnp.arange(MOST, dtype=jnp.int32)
    slot_of = (pack_index - own_index) % loaders
    source_live = positions[None, :] < patch_counts[:, None]
    source = pixels.reshape(IMG_LOAD, MOST, PATCH)
    source = jnp.where(source_live[:, :, None], source, jnp.zeros_like(source))
    outgoing = jnp.dot(
        source.reshape(IMG_LOAD * MOST, PATCH), embed_cols, preferred_element_type=jnp.float32
    )
    outgoing = outgoing.astype(jnp.bfloat16).reshape(IMG_LOAD, MOST, features)
    slot_pieces = []
    slot_sizes = []
    for slot_step in range(REACH):
        chosen = slot_of == slot_step
        slot_piece = jnp.sum(
            jnp.where(chosen[:, None, None], outgoing, jnp.zeros_like(outgoing)), axis=0
        )
        size_now = jnp.sum(jnp.where(chosen, patch_counts, 0)).astype(jnp.bfloat16)
        if slot_step > 0:
            slot_piece, size_now = from_behind((slot_piece, size_now), "dp", slot_step)
        slot_pieces.append(slot_piece)
        slot_sizes.append(size_now)
    arrived = jnp.stack(slot_pieces)
    counts_here = jnp.stack(slot_sizes).astype(jnp.int32)
    live_rows = (positions[None, :] < counts_here[:, None]).reshape(pack_rows)
    embedded = arrived.reshape(pack_rows, features)
    wide_rows = embedded.astype(jnp.float32)
    row_sums, row_squares = lax.psum(
        (jnp.sum(wide_rows, axis=1), jnp.sum(wide_rows * wide_rows, axis=1)), "mp"
    )
    row_mean = (row_sums / D)[:, None]
    row_var = (row_squares / D)[:, None] - row_mean * row_mean
    row_scale = lax.rsqrt(row_var + EPS)
    unit_rows = (wide_rows - row_mean) * row_scale
    normed = (unit_rows * norm_gain).astype(jnp.bfloat16)
    full_rows = lax.all_gather(normed, "mp", axis=1, tiled=True)
    query_full, key_full = (
        lax.all_gather(query_weight, "dp", axis=0, tiled=True),
        lax.all_gather(key_weight, "dp", axis=0, tiled=True),
    )
    queries = jnp.dot(full_rows, query_full, preferred_element_type=jnp.float32)
    key_rows = jnp.dot(full_rows, key_full, preferred_element_type=jnp.float32)
    query_unit, query_scale = head_norm(queries, heads_here, HD)
    key_unit, key_scale = head_norm(key_rows, heads_here, HD)
    query_hat = (query_unit * query_gain).astype(jnp.bfloat16)
    key_hat = (key_unit * key_gain).astype(jnp.bfloat16)
    blocks = 1
    segment = (jnp.arange(pack_rows, dtype=jnp.int32) // MOST)[None, :]
    head_values = normed.reshape(blocks, pack_rows, heads_here, group_width)[:, :, :, :HD]
    blended, grad_values, grad_query, grad_key = attend(
        query_hat.reshape(blocks, pack_rows, heads_here, HD),
        key_hat.reshape(blocks, pack_rows, heads_here, HD),
        head_values,
        cotangent.reshape(blocks, pack_rows, heads_here, HD),
        segment,
        live_rows.reshape(blocks, pack_rows),
        HD,
    )
    attended = blended.reshape(pack_rows, heads_here * HD).astype(jnp.bfloat16)
    grad_values = grad_values.reshape(pack_rows, heads_here, HD)
    grad_values = jnp.concatenate(
        [grad_values, jnp.zeros((pack_rows, heads_here, group_width - HD), jnp.float32)], axis=2
    )
    grad_query = head_back(
        grad_query.reshape(pack_rows, heads_here, HD), query_unit, query_scale, query_gain
    )
    grad_key = head_back(grad_key.reshape(pack_rows, heads_here, HD), key_unit, key_scale, key_gain)
    query_low = grad_query.reshape(pack_rows, heads_here * HD).astype(jnp.bfloat16)
    key_low = grad_key.reshape(pack_rows, heads_here * HD).astype(jnp.bfloat16)
    contract = (((1,), (1,)), ((), ()))
    partial_rows = lax.dot_general(
        query_low, query_full, contract, preferred_element_type=jnp.float32
    )
    partial_rows = partial_rows + lax.dot_general(
        key_low, key_full, contract, preferred_element_type=jnp.float32
    )
    grad_normed = lax.psum_scatter(
        partial_rows.astype(jnp.bfloat16), "mp", scatter_dimension=1, tiled=True
    ).astype(jnp.float32) + grad_values.reshape(pack_rows, features)
    grad_unit = grad_normed * norm_gain
    unit_sum, cross_sum = lax.psum(
        (jnp.sum(grad_unit, axis=1), jnp.sum(grad_unit * unit_rows, axis=1)), "mp"
    )
    grad_wide = row_scale * (
        grad_unit - (unit_sum / D)[:, None] - unit_rows * (cross_sum / D)[:, None]
    )
    grad_embedded = grad_wide.astype(jnp.bfloat16)
    contract_rows = (((0,), (0,)), ((), ()))
    returned = []
    for slot_step in range(REACH):
        slot_grad = grad_embedded[slot_step * MOST : (slot_step + 1) * MOST]
        if slot_step > 0:
            slot_grad = from_behind(slot_grad, "dp", -slot_step)
        returned.append(slot_grad)
    returned = jnp.stack(returned)
    picker = (slot_of[:, None] == jnp.arange(REACH, dtype=jnp.int32)[None, :]).astype(jnp.bfloat16)
    image_grads = jnp.einsum(
        "ir,rmf->imf", picker, returned, preferred_element_type=jnp.float32
    ).astype(jnp.bfloat16)
    partial_embed = lax.dot_general(
        source.reshape(IMG_LOAD * MOST, PATCH),
        image_grads.reshape(IMG_LOAD * MOST, features),
        contract_rows,
        preferred_element_type=jnp.float32,
    )
    embed_grad = lax.psum_scatter(partial_embed, "dp", scatter_dimension=1, tiled=True)
    return (attended, embed_grad.reshape(PATCH, 1, features // loaders))


def solution(mesh):
    placed = (
        P("dp", None),
        P("dp"),
        P("dp"),
        P(None, "mp", "dp"),
        P("mp"),
        P("dp", "mp"),
        P("dp", "mp"),
        P(),
        P(),
        P("dp", "mp"),
    )
    return jax.shard_map(
        per_device,
        mesh=mesh,
        in_specs=placed,
        out_specs=(P("dp", "mp"), P(None, "mp", "dp")),
        check_vma=False,
    )
```

profile of v0, /device:TPU:32, one launch (start us, length us, event | category | flops | bytes accessed | tf_op | source)
XLA Modules:
  0.0 583.8 jit_solution(13229053299053704468)
XLA Ops:
  10.2 79.5 %all-gather.5.cloned.1.call-done = bf16[588,1,1536]{0,2,1:T(8,128)(2,1)} async-done(((bf16[588,1,24]{0,2,1:T(8,128)(2,1)}), bf16[588,1,1536]{0,2,1:T(8,128)(2,1)}) %all-gather.5.cloned.1.call-update) | async-done | bytes 1806352 | tf_op jit(solution)/shard_map/all_gather | solution.py:88
  89.7 2.5 convolution_convert_fusion.1
  92.7 2.0 collective-permute-start.2
  96.3 8.1 %collective-permute-done.2 = bf16[48,1536]{1,0:T(8,128)(2,1)S(1)} collective-permute-done((bf16[48,1536]{1,0:T(8,128)(2,1)S(1)}, bf16[48,1536]{1,0:T(8,128)(2,1)S(1)}, u32[]{:S(2)}, u32[]{:S(2)}) %collective-permute-start.2) | collective-permute-done | bytes 147488 | tf_op jit(solution)/shard_map/ppermute | solution.py:21
  106.2 10.4 %all-reduce.3 = (f32[192]{0:T(256)S(1)}, f32[192]{0:T(256)S(1)}) all-reduce(f32[192]{0:T(256)S(1)} %reduce_sum.221, f32[192]{0:T(256)S(1)} %reduce_sum.219), channel_id=1, replica_groups=mesh['dp'=64,'mp'=4] {'mp'}, use_global_device_ids=true, to_apply=%region_7.8 | all-reduce | flops 384 | bytes 3072 | tf_op jit(solution)/shard_map/psum | solution.py:115
  121.9 3.1 collective-permute-start.4
  125.6 2.4 collective-permute-start.3
  128.8 2.0 maximum_convert_fusion.1
  131.7 1.5 reshape.472
  136.8 14.3 %all-gather.7.cloned.1.call-done = bf16[192,6144]{1,0:T(8,128)(2,1)} async-done(((bf16[192,1536]{1,0:T(8,128)(2,1)}), bf16[192,6144]{1,0:T(8,128)(2,1)}) %all-gather.7.cloned.1.call-update) | async-done | bytes 2359312 | tf_op jit(solution)/shard_map/all_gather | solution.py:123
  151.1 87.6 %all-gather.11.cloned.1.call-done = bf16[6144,768]{1,0:T(8,128)(2,1)} async-done(((bf16[96,768]{1,0:T(8,128)(2,1)}), bf16[6144,768]{1,0:T(8,128)(2,1)}) %all-gather.11.cloned.1.call-update) | async-done | bytes 9437200 | tf_op jit(solution)/shard_map/all_gather | solution.py:126
  238.7 6.4 %fusion.78 = f32[192,768]{1,0:T(8,128)S(1)} fusion(bf16[192,6144]{1,0:T(8,128)(2,1)} %all-gather.7.cloned.1.call-done, bf16[6144,768]{1,0:T(8,128)(2,1)} %all-gather.11.cloned.1.call-done), kind=kOutput, calls=%fused_computation.142 | convolution fusion | flops 1811939328 | bytes 12386304 | tf_op jit(solution)/shard_map/dot_general | solution.py:129
  245.2 78.1 %all-gather.9.cloned.1.call-done = bf16[6144,768]{1,0:T(8,128)(2,1)} async-done(((bf16[96,768]{1,0:T(8,128)(2,1)}), bf16[6144,768]{1,0:T(8,128)(2,1)}) %all-gather.9.cloned.1.call-update) | async-done | bytes 9437200 | tf_op jit(solution)/shard_map/all_gather | solution.py:125
  323.3 6.4 %fusion.77 = f32[192,768]{1,0:T(8,128)S(1)} fusion(bf16[192,6144]{1,0:T(8,128)(2,1)} %all-gather.7.cloned.1.call-done, bf16[6144,768]{1,0:T(8,128)(2,1)} %all-gather.9.cloned.1.call-done), kind=kOutput, calls=%fused_computation.141 | convolution fusion | flops 1811939328 | bytes 12386304 | tf_op jit(solution)/shard_map/dot_general | solution.py:128
  330.7 2.7 fusion.69
  337.4 2.9 fusion.72
  340.4 4.4 fusion.34
  344.8 4.8 fusion.35
  352.6 1.4 copy.110
  354.7 1.5 copy.118
  357.4 1.4 copy.116
  358.9 1.5 copy.115
  361.8 7.2 %fusion.39 = f32[192,6144]{1,0:T(8,128)S(1)} fusion(bf16[6144,768]{1,0:T(8,128)(2,1)} %all-gather.9.cloned.1.call-done, f32[24,8,6,128]{3,2,1,0:T(8,128)S(1)} %bitcast.221, f32[192,768]{1,0:T(8,128)S(1)} %fusion.77, f32[24,8,6,128]{3,2,1,0:T(8,128)S(1)} %bitcast.222, f32[24,8,6,128]{3,2,1,0:T(8,128)S(1)} %bitcast.223, f32[24,8,6,128]{3,2,1,0:T(8,128)S(1)} %bitcast.225, ...), kind=kOutput, calls=%fused_computation.76 | convolution fusion | flops 1813118976 | bytes 17697792 | tf_op jit(solution)/shard_map/dot_general | solution.py:158
  370.4 8.6 %fusion.1 = bf16[192,6144]{1,0:T(8,128)(2,1)} fusion(f32[192,6144]{1,0:T(8,128)S(1)} %fusion.39, bf16[6144,768]{1,0:T(8,128)(2,1)} %all-gather.11.cloned.1.call-done, f32[24,8,6,128]{3,2,1,0:T(8,128)S(1)} %bitcast.216, f32[192,768]{1,0:T(8,128)S(1)} %fusion.78, f32[24,8,6,128]{3,2,1,0:T(8,128)S(1)} %bitcast.217, f32[24,8,6,128]{3,2,1,0:T(8,128)S(1)} %bitcast.218, ...), kind=kOutput, calls=%fused_computation.2 | convolution fusion | flops 1815478272 | bytes 20057088 | tf_op jit(solution)/shard_map/dot_general | solution.py:161
  381.6 29.2 %reduce-scatter.5.cloned.1.call-done = bf16[192,1536]{1,0:T(8,128)(2,1)} async-done(((bf16[192,6144]{1,0:T(8,128)(2,1)}), bf16[192,1536]{1,0:T(8,128)(2,1)}) %reduce-scatter.5.cloned.1.call-update) | async-done | bytes 589840 | tf_op jit(solution)/shard_map/reduce_scatter | solution.py:164
  410.8 1.5 fusion.37
  412.3 8.6 %all-reduce.2 = (f32[192]{0:T(256)S(1)}, f32[192]{0:T(256)S(1)}) all-reduce(f32[192]{0:T(256)S(1)} %get-tuple-element.3, f32[192]{0:T(256)S(1)} %get-tuple-element.2), channel_id=1, replica_groups=mesh['dp'=64,'mp'=4] {'mp'}, use_global_device_ids=true, to_apply=%region_26.27 | all-reduce | flops 384 | bytes 3072 | tf_op jit(solution)/shard_map/psum | solution.py:168
  421.3 2.9 collective-permute-start.8
  425.6 2.5 collective-permute-start.6
  429.0 3.3 collective-permute-done.7
  433.4 2.8 convolution_bitcast_fusion
  439.2 137.8 %reduce-scatter.7.cloned.1.call-done = f32[588,24]{0,1:T(8,128)} async-done(((f32[588,1536]{0,1:T(8,128)}), f32[588,24]{0,1:T(8,128)}) %reduce-scatter.7.cloned.1.call-update) | async-done | bytes 56464
  (152 shorter events, 37.3 us)
Async XLA Ops:
  7.2 128.2 %copy-start = (bf16[192,768]{1,0:T(8,128)(2,1)S(1)}, bf16[192,768]{1,0:T(8,128)(2,1)}, u32[]{:S(2)}) copy-start(bf16[192,768]{1,0:T(8,128)(2,1)} %param.19) | copy-start | bytes 884740
  7.2 82.5 %all-gather.5.cloned.1.call-start = ((), (), s32[]{:S(2)}) async-start(), calls=%async_computation.2 | async-start | bytes 1996800 | tf_op jit(solution)/shard_map/all_gather | solution.py:88
  7.9 143.2 %all-gather.7.cloned.1.call-start = ((), (), s32[]{:S(2)}) async-start(), calls=%async_computation.3 | async-start | bytes 2949120 | tf_op jit(solution)/shard_map/all_gather | solution.py:123
  10.2 81.9 %copy-start.24 = (s32[3]{0:T(128)}, s32[3]{0:T(128)S(1)}, u32[]{:S(2)}) copy-start(s32[3]{0:T(128)S(1)} %get-tuple-element.28) | copy-start | bytes 40
  92.7 11.7 %collective-permute-start.2 = (bf16[48,1536]{1,0:T(8,128)(2,1)S(1)}, bf16[48,1536]{1,0:T(8,128)(2,1)S(1)}, u32[]{:S(2)}, u32[]{:S(2)}) collective-permute-start(bf16[48,1536]{1,0:T(8,128)(2,1)S(1)} %get-tuple-element.15), channel_id=1, source_target_pairs={{244,0},{248,4},{252,8},{0,12},{4,16},{8,20},{12,24},{16,28},{20,3... | collective-permute-start | bytes 442376 | tf_op jit(solution)/shard_map/ppermute | solution.py:21
  94.8 9.6 %collective-permute-start.1 = (bf16[48,1536]{1,0:T(8,128)(2,1)S(1)}, bf16[48,1536]{1,0:T(8,128)(2,1)S(1)}, u32[]{:S(2)}, u32[]{:S(2)}) collective-permute-start(bf16[48,1536]{1,0:T(8,128)(2,1)S(1)} %get-tuple-element.16), channel_id=1, source_target_pairs={{248,0},{252,4},{0,8},{4,12},{8,16},{12,20},{16,24},{20,28},{24,32... | collective-permute-start | bytes 442376 | tf_op jit(solution)/shard_map/ppermute | solution.py:21
  95.4 10.3 %collective-permute-start = (bf16[48,1536]{1,0:T(8,128)(2,1)S(1)}, bf16[48,1536]{1,0:T(8,128)(2,1)S(1)}, u32[]{:S(2)}, u32[]{:S(2)}) collective-permute-start(bf16[48,1536]{1,0:T(8,128)(2,1)S(1)} %get-tuple-element.17), channel_id=1, source_target_pairs={{252,0},{0,4},{4,8},{8,12},{12,16},{16,20},{20,24},{24,28},{28,32}... | collective-permute-start | bytes 442376 | tf_op jit(solution)/shard_map/ppermute | solution.py:21
  105.7 10.9 %copy-start.12 = (f32[1536]{0:T(1024)S(1)}, f32[1536]{0:T(1024)}, u32[]{:S(2)}) copy-start(f32[1536]{0:T(1024)} %param.14) | copy-start | bytes 18436
  116.6 17.8 %copy-start.13 = (f32[192]{0:T(256)}, f32[192]{0:T(256)S(1)}, u32[]{:S(2)}) copy-start(f32[192]{0:T(256)S(1)} %get-tuple-element.38) | copy-start | bytes 2308
  116.6 17.8 %copy-start.17 = (f32[192]{0:T(256)}, f32[192]{0:T(256)S(1)}, u32[]{:S(2)}) copy-start(f32[192]{0:T(256)S(1)} %get-tuple-element.37) | copy-start | bytes 2308
  116.7 12.1 %copy-start.30 = (f32[128]{0:T(128)S(1)}, f32[128]{0:T(128)}, u32[]{:S(2)}) copy-start(f32[128]{0:T(128)} %param.17) | copy-start | bytes 1540
  116.7 12.1 %copy-start.28 = (f32[128]{0:T(128)S(1)}, f32[128]{0:T(128)}, u32[]{:S(2)}) copy-start(f32[128]{0:T(128)} %param.18) | copy-start | bytes 1540
  117.8 120.9 %all-gather.11.cloned.1.call-start = ((), (), s32[]{:S(2)}) async-start(), calls=%async_computation.5 | async-start | bytes 9584640 | tf_op jit(solution)/shard_map/all_gather | solution.py:126
  118.5 204.8 %all-gather.9.cloned.1.call-start = ((), (), s32[]{:S(2)}) async-start(), calls=%async_computation.4 | async-start | bytes 9584640 | tf_op jit(solution)/shard_map/all_gather | solution.py:125
  119.1 291.7 %reduce-scatter.5.cloned.1.call-start = ((), (), s32[]{:S(2)}) async-start(), calls=%async_computation.6 | async-start | bytes 2949120 | tf_op jit(solution)/shard_map/reduce_scatter | solution.py:164
  119.9 8.9 %collective-permute-start.5 = (bf16[]{:T(256)}, bf16[]{:T(256)}, u32[]{:S(2)}, u32[]{:S(2)}) collective-permute-start(bf16[]{:T(256)} %convert_element_type.123), channel_id=1, source_target_pairs={{244,0},{248,4},{252,8},{0,12},{4,16},{8,20},{12,24},{16,28},{20,3... | collective-permute-start | bytes 14 | tf_op jit(solution)/shard_map/ppermute | solution.py:21
  121.9 6.9 %collective-permute-start.4 = (bf16[]{:T(256)}, bf16[]{:T(256)}, u32[]{:S(2)}, u32[]{:S(2)}) collective-permute-start(bf16[]{:T(256)} %convert_element_type.122), channel_id=1, source_target_pairs={{248,0},{252,4},{0,8},{4,12},{8,16},{12,20},{16,24},{20,28},{24,32... | collective-permute-start | bytes 14 | tf_op jit(solution)/shard_map/ppermute | solution.py:21
  125.6 3.2 collective-permute-start.3
  128.1 6.4 %copy-start.15 = (f32[6,128]{1,0:T(8,128)}, f32[6,128]{1,0:T(8,128)S(1)}, u32[]{:S(2)}) copy-start(f32[6,128]{1,0:T(8,128)S(1)} %slice.21) | copy-start | bytes 9220
  337.4 3.0 copy-start.23
  337.4 3.0 copy-start.29
  337.4 3.0 copy-start.31
  340.4 4.4 copy-start.19
  361.8 7.2 %copy-start.8 = (f32[192,6]{1,0:T(8,128)S(1)}, f32[192,6]{1,0:T(8,128)}, u32[]{:S(2)}) copy-start(f32[192,6]{1,0:T(8,128)} %copy.118) | copy-start | bytes 13828
  361.8 7.5 %copy-start.7 = (f32[192,6]{1,0:T(8,128)S(1)}, f32[192,6]{1,0:T(8,128)}, u32[]{:S(2)}) copy-start(f32[192,6]{1,0:T(8,128)} %copy.130) | copy-start | bytes 13828
  379.1 197.9 %reduce-scatter.7.cloned.1.call-start = ((), (), s32[]{:S(2)}) async-start(), calls=%async_computation.7 | async-start | bytes 3993600
  410.8 10.1 %copy-start.3 = (bf16[192,1536]{1,0:T(8,128)(2,1)S(1)}, bf16[192,1536]{1,0:T(8,128)(2,1)}, u32[]{:S(2)}) copy-start(bf16[192,1536]{1,0:T(8,128)(2,1)} %reduce-scatter.5.cloned.1.call-done) | copy-start | bytes 1769476
  410.8 10.1 %copy-start.14 = (f32[192]{0:T(256)S(1)}, f32[192]{0:T(256)}, u32[]{:S(2)}) copy-start(f32[192]{0:T(256)} %copy-done.13) | copy-start | bytes 2308
  421.2 11.3 %copy-start.25 = (s32[3]{0:T(128)S(1)}, s32[3]{0:T(128)}, u32[]{:S(2)}) copy-start(s32[3]{0:T(128)} %copy-done.24) | copy-start | bytes 40
  421.3 7.7 %collective-permute-start.8 = (bf16[48,1536]{1,0:T(8,128)(2,1)S(1)}, bf16[48,1536]{1,0:T(8,128)(2,1)S(1)}, u32[]{:S(2)}, u32[]{:S(2)}) collective-permute-start(bf16[48,1536]{1,0:T(8,128)(2,1)S(1)} %get-tuple-element.30), channel_id=1, source_target_pairs={{12,0},{16,4},{20,8},{24,12},{28,16},{32,20},{36,24},{40,28},{44,3... | collective-permute-start | bytes 442376 | tf_op jit(solution)/shard_map/ppermute | solution.py:21
  424.2 8.0 %collective-permute-start.7 = (bf16[48,1536]{1,0:T(8,128)(2,1)S(1)}, bf16[48,1536]{1,0:T(8,128)(2,1)S(1)}, u32[]{:S(2)}, u32[]{:S(2)}) collective-permute-start(bf16[48,1536]{1,0:T(8,128)(2,1)S(1)} %get-tuple-element.31), channel_id=1, source_target_pairs={{8,0},{12,4},{16,8},{20,12},{24,16},{28,20},{32,24},{36,28},{40,32... | collective-permute-start | bytes 442376 | tf_op jit(solution)/shard_map/ppermute | solution.py:21
  425.6 6.9 %collective-permute-start.6 = (bf16[48,1536]{1,0:T(8,128)(2,1)S(1)}, bf16[48,1536]{1,0:T(8,128)(2,1)S(1)}, u32[]{:S(2)}, u32[]{:S(2)}) collective-permute-start(bf16[48,1536]{1,0:T(8,128)(2,1)S(1)} %get-tuple-element.32), channel_id=1, source_target_pairs={{4,0},{8,4},{12,8},{16,12},{20,16},{24,20},{28,24},{32,28},{36,32}... | collective-permute-start | bytes 442376 | tf_op jit(solution)/shard_map/ppermute | solution.py:21
  (17 other events, 21.0 us)
Sparse Core Ops, SparseCore 0:
  10.7 78.9 all-gather.4
  117.9 33.1 all-gather.6
  153.8 84.8 all-gather.10
  241.3 81.9 all-gather.8
  379.2 31.5 reduce-scatter.4
  436.3 140.5 reduce-scatter.6
where the time goes:
time: 586 us; the launch traced here: 584 us
  waiting for transfers between devices  442 us (75%)
  matrix products  48.7 us (8%)
  local copies, waits for them, and re-layouts  25.5 us (4%)
  blocking collectives  19 us (3%)
  starting transfers between devices  17.5 us (3%)
  between operations  17.2 us (3%)
  other arithmetic  13.6 us (2%)
    unnamed x7, waiting for transfers between devices  140 us
    all_gather x1, waiting for transfers between devices, per_device(): lax.all_gather(key_weight, 'dp', axis=0, tiled=True)  87.6 us
    all_gather x1, waiting for transfers between devices, per_device(): lax.all_gather(embed_weight, 'dp', axis=2, tiled=True)  79.5 us
    all_gather x1, waiting for transfers between devices, per_device(): lax.all_gather(query_weight, 'dp', axis=0, tiled=True)  78.1 us
    reduce_scatter x1, waiting for transfers between devices, per_device(): lax.psum_scatter(partial_rows.astype(jnp.bfloat16), 'mp', scatter_dimensi...  29.2 us
    ppermute x9, starting transfers between devices, from_behind(): return lax.ppermute(block, axis, route)  17.3 us
    all_gather x1, waiting for transfers between devices, per_device(): full_rows = lax.all_gather(normed, 'mp', axis=1, tiled=True)  14.3 us
    ppermute x9, waiting for transfers between devices, from_behind(): return lax.ppermute(block, axis, route)  13.8 us
  transfers between devices with their start and end apart: 15, of which 11 were waited for; matrix products, arithmetic and copies ran while one was open for 3% of the time, Pallas kernels for 0%

commit v1 on v0

v1 whole, which is shorter than its diff:
```python
import jax
import jax.numpy as jnp
from jax import lax
from jax.experimental import pallas as pl
from jax.experimental.pallas import tpu as pltpu
from jax.sharding import PartitionSpec as P

D = 6144
HEADS = 24
HD = 128
PATCH = 588
MOST = 48
IMG_LOAD = 3
REACH = 4
EPS = 1e-06

NY, NZ, NC, NX = 4, 8, 2, 4
NDP = NY * NZ * NC
FX = D // NX
FB = FX // NC
HC = HEADS // NX // NC
HW = HC * HD
ROWS = NC * IMG_LOAD * MOST
EROWS = ROWS + 16
STRIP = FB // NZ
PACK = REACH * MOST
PIECE = FX // NDP
YROWS = NZ * PIECE
NT = (((1,), (1,)), ((), ()))
TN = (((0,), (0,)), ((), ()))
F32 = jnp.float32
BF16 = jnp.bfloat16
HIGH = lax.Precision.HIGHEST


def dot(a, b, dims=(((1,), (0,)), ((), ()))):
    return lax.dot_general(a, b, dims, preferred_element_type=F32)


def dp_index(y, z, c):
    return ((y % NY) * NZ + z % NZ) * NC + c


DP_ALL = [(y, z, c) for y in range(NY) for z in range(NZ) for c in range(NC)]


def core_swap(v):
    return lax.ppermute(v, "dp", [(i, i ^ 1) for i in range(NDP)])


def z_shift(v, k):
    return lax.ppermute(v, "dp", [(dp_index(y, z, c), dp_index(y, z + k, c)) for y, z, c in DP_ALL])


def y_shift(v, k):
    return lax.ppermute(v, "dp", [(dp_index(y, z, c), dp_index(y + k, z, c)) for y, z, c in DP_ALL])


def x_shift(v, k):
    return lax.ppermute(v, "mp", [(i, (i + k) % NX) for i in range(NX)])


def chip_shift(v, k):
    return lax.ppermute(v, "dp", [(i, (i + NC * k) % NDP) for i in range(NDP)])


def by_core(core, mine, other, axis):
    return jnp.where(
        core == 0,
        jnp.concatenate([mine, other], axis=axis),
        jnp.concatenate([other, mine], axis=axis),
    )


def turn(pieces, start, axis):
    n = len(pieces)
    double = jnp.concatenate(list(pieces) + list(pieces), axis=axis)
    size = pieces[0].shape[axis]
    return lax.dynamic_slice_in_dim(double, start * size, n * size, axis=axis)


def vmem(n):
    return [pl.BlockSpec(memory_space=pltpu.VMEM)] * n


def embed_kernel(place, pix, w0, w1, w2, w3, gain, out, weights):
    y = place[1]
    for k, piece in enumerate((w0, w1, w2, w3)):
        at = pl.multiple_of(lax.rem(y + k, NY) * YROWS, YROWS)
        weights[pl.ds(at, YROWS), :] = piece[...]
    out[:ROWS, :] = dot(pix[...], weights[...], NT).astype(BF16)
    full = gain[...]
    high = full.astype(BF16)
    rest = full - high.astype(F32)
    mid = rest.astype(BF16)
    low = (rest - mid.astype(F32)).astype(BF16)
    row = lax.broadcasted_iota(jnp.int32, (16, FB), 0)
    out[ROWS:, :] = jnp.where(
        row == 0,
        high.astype(F32),
        jnp.where(row == 1, mid.astype(F32), jnp.where(row == 2, low.astype(F32), 0.0)),
    ).astype(BF16)


def embed(place, pix, pieces, gain):
    return pl.pallas_call(
        embed_kernel,
        out_shape=jax.ShapeDtypeStruct((EROWS, FB), BF16),
        in_specs=[pl.BlockSpec(memory_space=pltpu.SMEM)] + vmem(6),
        out_specs=pl.BlockSpec(memory_space=pltpu.VMEM),
        scratch_shapes=[pltpu.VMEM((FB, PATCH), BF16)],
        compiler_params=pltpu.CompilerParams(vmem_limit_bytes=24 * 2**20),
        cost_estimate=pl.CostEstimate(
            flops=2 * ROWS * FB * PATCH, bytes_accessed=2000000, transcendentals=0
        ),
        name="embed",
    )(place, pix, *pieces, gain)


def gain_of(rows):
    wide = rows.astype(F32)
    return wide[0:1] + wide[1:2] + wide[2:3]


def head_norm(values):
    center = jnp.mean(values, axis=1, keepdims=True)
    spread = jnp.mean(values * values, axis=1, keepdims=True) - center * center
    inv = lax.rsqrt(spread + EPS)
    return (values - center) * inv, inv


def head_back(grad_hat, unit, inv, gain):
    t = grad_hat * gain
    mean_t = jnp.mean(t, axis=1, keepdims=True)
    second = jnp.mean(t * unit, axis=1, keepdims=True)
    return inv * (t - mean_t - unit * second)


def lanes_sum(v):
    total = v[:, :128]
    for k in range(1, v.shape[1] // 128):
        total = total + v[:, k * 128 : (k + 1) * 128]
    return total


def layer_kernel(*refs):
    place, counts = refs[:2]
    e_refs = refs[2:10]
    a_refs = refs[10:15]
    b_refs = refs[15:24]
    pick, cot, q_gain, k_gain = refs[24:28]
    att, own_out, other_out, stats_out, ms_out = refs[28:33]
    e, w, normed, acc, grad, grad_v, acc1, acc2, sems = refs[33:]
    x, y, z, c = place[0], place[1], place[2], place[3]

    copies = []

    def go(src, dst):
        copy = pltpu.make_async_copy(src, dst, sems.at[len(copies)])
        copy.start()
        copies.append(copy)

    for k in range(NX):
        xk = lax.rem(x + k, NX)
        go(e_refs[k], e.at[2 * xk + c])
        go(e_refs[NX + k], e.at[2 * xk + 1 - c])
    n_e = len(copies)
    first = pl.ds(0, HW)
    second = pl.ds(HW, HW)
    for k in range(3):
        yk = lax.rem(y + (0, NY - 1, 1)[k], NY)
        go(a_refs[k], w.at[pl.ds(2 * yk, 2), :, first])
    y2 = lax.rem(y + 2, NY)
    go(a_refs[3], w.at[2 * y2, :, first])
    go(a_refs[4], w.at[2 * y2 + 1, :, first])
    for k in range(7):
        zk = lax.rem(z + (0, NZ - 1, 1, NZ - 2, 2, NZ - 3, 3)[k], NZ)
        at = pl.multiple_of(zk * STRIP, STRIP)
        go(b_refs[k], w.at[:, pl.ds(at, STRIP), second])
    z4 = pl.multiple_of(lax.rem(z + 4, NZ) * STRIP, STRIP)
    go(b_refs[7], w.at[pl.ds(0, 4), pl.ds(z4, STRIP), second])
    go(b_refs[8], w.at[pl.ds(4, 4), pl.ds(z4, STRIP), second])

    for copy in copies[:n_e]:
        copy.wait()
    acc1[...] = jnp.zeros_like(acc1)
    acc2[...] = jnp.zeros_like(acc2)

    def sums(b, carry):
        wide = e[b, :ROWS, :].astype(F32)
        acc1[...] += lanes_sum(wide)
        acc2[...] += lanes_sum(wide * wide)
        return carry

    lax.fori_loop(0, 8, sums, 0)
    mean = jnp.sum(acc1[...], axis=1, keepdims=True) * (1.0 / D)
    square = jnp.sum(acc2[...], axis=1, keepdims=True) * (1.0 / D)
    scale = lax.rsqrt(square - mean * mean + EPS)
    lane = lax.broadcasted_iota(jnp.int32, (ROWS, 128), 1)
    ms_out[...] = jnp.where(lane == 0, mean, scale)

    def norm(b, carry):
        wide = e[b, :ROWS, :].astype(F32)
        gain = gain_of(e[b, ROWS:, :])
        normed[b] = ((wide - mean) * scale * gain).astype(BF16)
        return carry

    lax.fori_loop(0, 8, norm, 0)
    values = dot(normed[2 * x], pick[0]) + dot(normed[2 * x + 1], pick[1])
    values = values.astype(BF16)

    for copy in copies[n_e:]:
        copy.wait()
    acc[...] = jnp.zeros_like(acc)

    def project(b, carry):
        acc[...] += dot(normed[b], w[b])
        return carry

    lax.fori_loop(0, 8, project, 0)

    inv_root = HD ** (-0.5)
    span = 2 * MOST
    row = lax.broadcasted_iota(jnp.int32, (span, span), 0)
    col = lax.broadcasted_iota(jnp.int32, (span, span), 1)
    qg, kg = q_gain[...], k_gain[...]
    masks = []
    for g in range(ROWS // span):
        n0, n1 = counts[2 * g], counts[2 * g + 1]
        top_r = jnp.where(row < MOST, n0, n1 + MOST)
        top_c = jnp.where(col < MOST, n0, n1 + MOST)
        same = jnp.where(row < MOST, 0, 1) == jnp.where(col < MOST, 0, 1)
        masks.append(((row < top_r) & (col < top_c) & same, row[:, :1] < top_r[:, :1]))
    for h in range(HC):
        cols = slice(h * HD, (h + 1) * HD)
        kcols = slice(HW + h * HD, HW + (h + 1) * HD)
        q_unit, q_inv = head_norm(acc[:, cols])
        k_unit, k_inv = head_norm(acc[:, kcols])
        q_hat = (q_unit * qg).astype(BF16)
        k_hat = (k_unit * kg).astype(BF16)
        gq, gk = [], []
        for g in range(ROWS // span):
            rows = slice(g * span, (g + 1) * span)
            allowed, live = masks[g]
            q, k, v, go_ = q_hat[rows], k_hat[rows], values[rows, cols], cot[rows, cols]
            scores = dot(q, k, NT) * inv_root
            raised = jnp.where(allowed, jnp.exp(scores), 0.0)
            totals = jnp.sum(raised, axis=1, keepdims=True)
            totals = jnp.where(live, totals, 1.0)
            probs = raised / totals
            low = probs.astype(BF16)
            att[rows, cols] = dot(low, v).astype(BF16)
            g_probs = dot(go_, v, NT)
            grad_v[rows, cols] = dot(low, go_, TN).astype(BF16)
            g_scores = probs * (g_probs - jnp.sum(probs * g_probs, axis=1, keepdims=True))
            g_low = (g_scores * inv_root).astype(BF16)
            gq.append(dot(g_low, k))
            gk.append(dot(g_low, q, TN))
        grad[:, cols] = head_back(jnp.concatenate(gq, axis=0), q_unit, q_inv, qg).astype(BF16)
        grad[:, kcols] = head_back(jnp.concatenate(gk, axis=0), k_unit, k_inv, kg).astype(BF16)

    acc1[...] = jnp.zeros_like(acc1)
    acc2[...] = jnp.zeros_like(acc2)

    def back(k, core, out, with_values):
        b = 2 * lax.rem(x + k, NX) + core
        part = dot(grad[...], w[b], NT)
        if with_values:
            part = part + dot(grad_v[...], pick[core], NT)
        out[k] = part.astype(BF16)
        t = part * gain_of(e[b, ROWS:, :])
        unit = (e[b, :ROWS, :].astype(F32) - mean) * scale
        acc1[...] += lanes_sum(t)
        acc2[...] += lanes_sum(t * unit)

    for out, core in ((other_out, 1 - c), (own_out, c)):
        back(0, core, out, True)

        def step(k, carry, core=core, out=out):
            back(k, core, out, False)
            return carry

        lax.fori_loop(1, NX, step, 0)
    ones = jnp.ones((8, 128), F32)
    for k, part in enumerate((acc1, acc2)):
        stats_out[k * 8 : (k + 1) * 8, :] = lax.dot_general(
            ones, part[...], NT, preferred_element_type=F32, precision=HIGH
        )


def layer(place, counts, blocks, a_pieces, b_pieces, pick, cot, q_gain, k_gain):
    hbm = [pl.BlockSpec(memory_space=pl.ANY)]
    smem = [pl.BlockSpec(memory_space=pltpu.SMEM)]
    flops = 4 * ROWS * D * 2 * HW
    return pl.pallas_call(
        layer_kernel,
        out_shape=(
            jax.ShapeDtypeStruct((ROWS, HW), BF16),
            jax.ShapeDtypeStruct((NX, ROWS, FB), BF16),
            jax.ShapeDtypeStruct((NX, ROWS, FB), BF16),
            jax.ShapeDtypeStruct((16, ROWS), F32),
            jax.ShapeDtypeStruct((ROWS, 128), F32),
        ),
        in_specs=smem * 2 + hbm * 22 + vmem(4),
        out_specs=tuple(vmem(5)),
        scratch_shapes=[
            pltpu.VMEM((8, EROWS, FB), BF16),
            pltpu.VMEM((8, FB, 2 * HW), BF16),
            pltpu.VMEM((8, ROWS, FB), BF16),
            pltpu.VMEM((ROWS, 2 * HW), F32),
            pltpu.VMEM((ROWS, 2 * HW), BF16),
            pltpu.VMEM((ROWS, HW), BF16),
            pltpu.VMEM((ROWS, 128), F32),
            pltpu.VMEM((ROWS, 128), F32),
            pltpu.SemaphoreType.DMA((22,)),
        ],
        compiler_params=pltpu.CompilerParams(vmem_limit_bytes=48 * 2**20),
        cost_estimate=pl.CostEstimate(flops=flops, bytes_accessed=20000000, transcendentals=100000),
        name="layer",
    )(place, counts, *blocks, *a_pieces, *b_pieces, pick, cot, q_gain, k_gain)


def embed_back_kernel(
    place, own, got, r1, r2, r3, e_own, ms, s0, s1, s2, s3, pix, own_out, send_out, full
):
    y = place[1]
    part = own[...].astype(F32)
    for ref in (got, r1, r2, r3):
        part = part + ref[...].astype(F32)
    mean, scale = ms[:, 0:1], ms[:, 1:2]
    gain = gain_of(e_own[ROWS:, :])
    total = s0[...] + s1[...] + s2[...] + s3[...]
    row = lax.broadcasted_iota(jnp.int32, (16, 128), 0)
    columns = []
    for k in range(2):
        chooser = jnp.where(row == 8 * k, 1.0 / D, 0.0).astype(F32)
        columns.append(
            lax.dot_general(total, chooser, TN, preferred_element_type=F32, precision=HIGH)[:, :1]
        )
    t = part * gain
    unit = (e_own[:ROWS, :].astype(F32) - mean) * scale
    grad = (scale * (t - columns[0] - unit * columns[1])).astype(BF16)
    full[...] = dot(grad, pix[...], TN)
    for k in range(NY):
        at = pl.multiple_of(lax.rem(y + k, NY) * YROWS, YROWS)
        piece = full[pl.ds(at, YROWS), :]
        if k == 0:
            own_out[...] = piece
        else:
            send_out[k - 1] = piece.astype(BF16)


def embed_back(place, *args):
    return pl.pallas_call(
        embed_back_kernel,
        out_shape=(
            jax.ShapeDtypeStruct((YROWS, PATCH), F32),
            jax.ShapeDtypeStruct((NY - 1, YROWS, PATCH), BF16),
        ),
        in_specs=[pl.BlockSpec(memory_space=pltpu.SMEM)] + vmem(12),
        out_specs=tuple(vmem(2)),
        scratch_shapes=[pltpu.VMEM((FB, PATCH), F32)],
        compiler_params=pltpu.CompilerParams(vmem_limit_bytes=32 * 2**20),
        cost_estimate=pl.CostEstimate(
            flops=2 * ROWS * FB * PATCH, bytes_accessed=5000000, transcendentals=0
        ),
        name="embed_back",
    )(place, *args)


def per_device(
    pixels,
    patch_counts,
    pack_index,
    embed_weight,
    norm_gain,
    query_weight,
    key_weight,
    query_gain,
    key_gain,
    cotangent,
):
    d = lax.axis_index("dp")
    x = lax.axis_index("mp")
    c = d % NC
    z = (d // NC) % NZ
    y = d // (NC * NZ)
    place = jnp.stack([x, y, z, c]).astype(jnp.int32)

    strip = jnp.swapaxes(embed_weight.reshape(PATCH, PIECE), 0, 1)
    around = [strip] + [z_shift(strip, -k) for k in range(1, NZ)]
    embed_0 = turn(around, NZ - z, 0)
    embed_pieces = [embed_0] + [y_shift(embed_0, -k) for k in range(1, NY)]

    positions = jnp.arange(MOST, dtype=jnp.int32)
    slot_here = (pack_index - d) % NDP
    source = pixels.reshape(IMG_LOAD, MOST, PATCH)
    source = jnp.where(positions[None, :, None] < patch_counts[:, None, None], source, 0)
    facts = jnp.stack([patch_counts, slot_here], axis=1).astype(BF16)
    facts = jnp.broadcast_to(facts[:, None, :], (IMG_LOAD, MOST, 2))
    source = jnp.concatenate([source, facts], axis=2).reshape(IMG_LOAD * MOST, PATCH + 2)
    both = by_core(c, source, core_swap(source), 0)
    pix = both[:, :PATCH]
    facts = both[::MOST, PATCH:].astype(jnp.int32)
    counts, slots = facts[:, 0], facts[:, 1].reshape(NC, IMG_LOAD)

    def half(w, core):
        part = lax.dynamic_slice_in_dim(w, core * HW, HW, axis=1)
        part = part.reshape(2, NC, PIECE, HW).swapaxes(0, 1)
        return part.reshape(NC, 2 * PIECE, HW)

    mine = jnp.stack([half(query_weight, c), half(key_weight, c)])
    send = jnp.stack([half(query_weight, 1 - c), half(key_weight, 1 - c)])
    shard = by_core(c, mine, core_swap(send), 2)
    a0, b0 = shard[0], shard[1]

    al1, ar1 = z_shift(a0, 1), z_shift(a0, -1)
    al2, ar2 = z_shift(al1, 1), z_shift(ar1, -1)
    al3, ar3 = z_shift(al2, 1), z_shift(ar2, -1)
    al4 = z_shift(al3, 1)
    a_own = turn([a0, ar1, ar2, ar3, al4, al3, al2, al1], NZ - z, 1)
    a_low, a_high = y_shift(a_own, 1), y_shift(a_own, -1)
    a_pieces = [a_own, a_low, a_high, y_shift(a_low[0], 1), y_shift(a_high[1], -1)]

    b_own = turn([b0] + [y_shift(b0, -k) for k in range(1, NY)], NY - y, 0)
    bl1, br1 = z_shift(b_own, 1), z_shift(b_own, -1)
    bl2, br2 = z_shift(bl1, 1), z_shift(br1, -1)
    bl3, br3 = z_shift(bl2, 1), z_shift(br2, -1)
    bl4, br4 = z_shift(bl3[:4], 1), z_shift(br3[4:], -1)
    b_pieces = [b_own, bl1, br1, bl2, br2, bl3, br3, bl4, br4]

    gain_here = jnp.where(
        c == 0, norm_gain.reshape(-1, NC, PIECE)[:, 0], norm_gain.reshape(-1, NC, PIECE)[:, 1]
    ).reshape(1, FB)
    e_own = embed(place, pix, embed_pieces, gain_here)
    blocks = [e_own] + [x_shift(e_own, -k) for k in range(1, NX)]
    blocks = blocks + [core_swap(v) for v in blocks]

    cot_mine = lax.dynamic_slice_in_dim(cotangent, c * HW, HW, axis=1)
    cot_send = lax.dynamic_slice_in_dim(cotangent, (1 - c) * HW, HW, axis=1)
    packs = by_core(c, cot_mine[None], core_swap(cot_send)[None], 0)
    packs = packs.reshape(NC, REACH, MOST, HW)
    near = chip_shift(jnp.stack([packs[0, 1], packs[0, 2], packs[1, 2], packs[1, 3]]), -1)
    far = chip_shift(packs[0, 3], -2)
    slot_cot = (
        (packs[0, 0], packs[1, 1], near[1], near[3]),
        (packs[1, 0], near[0], near[2], far),
    )
    cot_rows = []
    for a in range(NC):
        for i in range(IMG_LOAD):
            row = jnp.zeros((MOST, HW), BF16)
            for s in range(REACH):
                row = jnp.where(slots[a, i] == s, slot_cot[a][s], row)
            cot_rows.append(row)
    cot = jnp.concatenate(cot_rows, axis=0)

    column = jnp.arange(HW, dtype=jnp.int32)[None, None, :]
    feature = (c * HC + column // HD) * (D // HEADS) + column % HD
    at = (feature // (NC * PIECE)) * PIECE + feature % PIECE
    part = (feature // PIECE) % NC
    pick = (
        (jnp.arange(FB, dtype=jnp.int32)[None, :, None] == at)
        & (jnp.arange(NC, dtype=jnp.int32)[:, None, None] == part)
    ).astype(BF16)

    att, own_grad, other_grad, stats, ms = layer(
        place,
        counts,
        blocks,
        a_pieces,
        b_pieces,
        pick,
        cot,
        query_gain.reshape(1, HD),
        key_gain.reshape(1, HD),
    )

    got = core_swap(other_grad)
    stats = stats + core_swap(stats)
    pair = [
        (own_grad[k].astype(F32) + got[k].astype(F32)).astype(BF16) for k in range(1, NX)
    ]
    arrived = [x_shift(pair[k - 1], k) for k in range(1, NX)]
    all_stats = [stats] + [x_shift(stats, k) for k in range(1, NX)]
    grad_own, grad_send = embed_back(
        place, own_grad[0], got[0], *arrived, e_own, ms, *all_stats, pix
    )
    total = grad_own
    for k in range(1, NY):
        total = total + y_shift(grad_send[k - 1], k).astype(F32)
    total = total.reshape(NZ, PIECE, PATCH)
    total = lax.dynamic_slice_in_dim(jnp.concatenate([total, total]), z, NZ, axis=0)
    embed_grad = total[0]
    low = total.astype(BF16)
    for k in range(1, NZ):
        embed_grad = embed_grad + z_shift(low[k], k).astype(F32)
    embed_grad = jnp.swapaxes(embed_grad, 0, 1).reshape(PATCH, 1, PIECE)

    shaped = att.reshape(NC, IMG_LOAD, MOST, HW)
    placed = []
    for a in range(NC):
        for s in range(REACH):
            row = jnp.zeros((MOST, HW), BF16)
            for i in range(IMG_LOAD):
                row = jnp.where(slots[a, i] == s, shaped[a, i], row)
            placed.append(row)
    near = chip_shift(jnp.stack([placed[2], placed[3], placed[5], placed[6]]), 1)
    far = chip_shift(placed[7], 2)
    packs = jnp.concatenate(
        [placed[0], near[2], near[0], far, placed[4], placed[1], near[3], near[1]], axis=0
    ).reshape(NC, PACK, HW)
    keep = jnp.where(c == 0, packs[0], packs[1])
    give = jnp.where(c == 0, packs[1], packs[0])
    attended = by_core(c, keep, core_swap(give), 1)
    return attended, embed_grad


def solution(mesh):
    placed = (
        P("dp", None),
        P("dp"),
        P("dp"),
        P(None, "mp", "dp"),
        P("mp"),
        P("dp", "mp"),
        P("dp", "mp"),
        P(),
        P(),
        P("dp", "mp"),
    )
    return jax.shard_map(
        per_device,
        mesh=mesh,
        in_specs=placed,
        out_specs=(P("dp", "mp"), P(None, "mp", "dp")),
        check_vma=False,
    )
```

time: 586 us -> 254 us (0.43)
  waiting for transfers between devices: 442 us -> 74.5 us
  starting transfers between devices: 17.5 us -> 113 us
  matrix products: 48.7 us -> 0 us
  Pallas kernels: 0 us -> 26.3 us
  blocking collectives: 19 us -> 0 us
  local copies, waits for them, and re-layouts: 25.5 us -> 10.4 us
    all_gather x4 -> x0, waiting for transfers between devices: 260 us -> none  [the longest x1 87.6 us: per_device(): lax.all_gather(key_weight, 'dp', axis=0, tiled=True)]
    unnamed x7 -> x0, waiting for transfers between devices: 140 us -> none
    ppermute x9 -> x65, starting transfers between devices: 17.3 us -> 113 us  [the longest x29 51.9 us: z_shift(): lax.ppermute(v, 'dp', [(dp_index(y, z, c), dp_index(y, z + k, c)) for y,...]
    ppermute x9 -> x65, waiting for transfers between devices: 13.8 us -> 74.5 us  [the longest x29 25.6 us: z_shift(): lax.ppermute(v, 'dp', [(dp_index(y, z, c), dp_index(y, z + k, c)) for y,...]
    dot_general x13 -> x0, matrix products: 48.7 us -> none  [the longest x1 8.59 us: per_device(): lax.dot_general(key_low, key_full, contract, preferred_element_type=jnp.f...]
    reduce_scatter x1 -> x0, waiting for transfers between devices: 29.2 us -> none  [per_device(): lax.psum_scatter(partial_rows.astype(jnp.bfloat16), 'mp', scatter_dimensi...]
    pallas_call x0 -> x3, Pallas kernels: none -> 26.3 us  [the longest x1 22.7 us: layer(): pl.pallas_call(layer_kernel, out_shape=(jax.ShapeDtypeStruct((ROWS, HW),...]
    psum x2 -> x0, blocking collectives: 19 us -> none  [the longest x1 10.4 us: per_device(): lax.psum((jnp.sum(wide_rows, axis=1), jnp.sum(wide_rows * wide_rows, axis...]
  transfers between devices with their start and end apart: 15 -> 65, of which waited for: 11 -> 17; matrix products, arithmetic and copies ran while one was open for 3% -> 7% of each run, Pallas kernels for 0% -> 1%
where the time goes in v1:
time: 254 us; the launch traced here: 249 us
  starting transfers between devices  113 us (44%)
  waiting for transfers between devices  74.5 us (29%)
  Pallas kernels  26.3 us (10%)
  between operations  16.9 us (7%)
  local copies, waits for them, and re-layouts  10.4 us (4%)
  other arithmetic  8.21 us (3%)
    ppermute x29, starting transfers between devices, z_shift(): lax.ppermute(v, 'dp', [(dp_index(y, z, c), dp_index(y, z + k, c)) for y,...  51.9 us
    ppermute x13, starting transfers between devices, y_shift(): lax.ppermute(v, 'dp', [(dp_index(y, z, c), dp_index(y + k, z, c)) for y,...  31.4 us
    ppermute x29, waiting for transfers between devices, z_shift(): lax.ppermute(v, 'dp', [(dp_index(y, z, c), dp_index(y, z + k, c)) for y,...  25.6 us
    ppermute x9, waiting for transfers between devices, x_shift(): return lax.ppermute(v, 'mp', [(i, (i + k) % NX) for i in range(NX)])  25 us
    pallas_call x1, Pallas kernels, layer(): pl.pallas_call(layer_kernel, out_shape=(jax.ShapeDtypeStruct((ROWS, HW),...  22.7 us
    ppermute x13, waiting for transfers between devices, y_shift(): lax.ppermute(v, 'dp', [(dp_index(y, z, c), dp_index(y + k, z, c)) for y,...  21.6 us
    ppermute x9, starting transfers between devices, x_shift(): return lax.ppermute(v, 'mp', [(i, (i + k) % NX) for i in range(NX)])  16.1 us
    ppermute x4, starting transfers between devices, chip_shift(): return lax.ppermute(v, 'dp', [(i, (i + NC * k) % NDP) for i in range(NDP)])  11.2 us
  transfers between devices with their start and end apart: 65, of which 17 were waited for; matrix products, arithmetic and copies ran while one was open for 7% of the time, Pallas kernels for 1%

profile of v1, /device:TPU:32, one launch (start us, length us, event | category | flops | bytes accessed | tf_op | source)
XLA Modules:
  0.0 248.8 jit_solution(3050634453704632027)
XLA Ops:
  2.6 4.5 %collective-permute-start.6 = (bf16[24,588]{1,0:T(8,128)(2,1)}, bf16[24,588]{1,0:T(8,128)(2,1)S(1)}, u32[]{:S(2)}, u32[]{:S(2)}) collective-permute-start(bf16[24,588]{1,0:T(8,128)(2,1)} %bitcast.258), channel_id=1, source_target_pairs={{0,16},{4,20},{8,24},{12,28},{16,32},{20,36},{24,40},{28,44},{32,4... | collective-permute-start | bytes 84680 | tf_op jit(solution)/shard_map/ppermute | solution.py:52
  17.6 3.6 %collective-permute-start.2 = (bf16[24,588]{1,0:T(8,128)(2,1)S(1)}, bf16[24,588]{1,0:T(8,128)(2,1)S(1)}, u32[]{:S(2)}, u32[]{:S(2)}) collective-permute-start(bf16[24,588]{1,0:T(8,128)(2,1)S(1)} %bitcast.262), channel_id=1, source_target_pairs={{0,48},{4,52},{8,56},{12,60},{16,0},{20,4},{24,8},{28,12},{32,16},... | collective-permute-start | bytes 84680 | tf_op jit(solution)/shard_map/ppermute | solution.py:52
  21.3 3.0 %collective-permute-done.2 = bf16[24,588]{1,0:T(8,128)(2,1)S(1)} collective-permute-done((bf16[24,588]{1,0:T(8,128)(2,1)S(1)}, bf16[24,588]{1,0:T(8,128)(2,1)S(1)}, u32[]{:S(2)}, u32[]{:S(2)}) %collective-permute-start.2) | collective-permute-done | bytes 28256 | tf_op jit(solution)/shard_map/ppermute | solution.py:52
  24.3 4.5 %collective-permute-start.3 = (bf16[24,588]{1,0:T(8,128)(2,1)S(1)}, bf16[24,588]{1,0:T(8,128)(2,1)S(1)}, u32[]{:S(2)}, u32[]{:S(2)}) collective-permute-start(bf16[24,588]{1,0:T(8,128)(2,1)S(1)} %bitcast.263), channel_id=1, source_target_pairs={{0,40},{4,44},{8,48},{12,52},{16,56},{20,60},{24,0},{28,4},{32,8},... | collective-permute-start | bytes 84680 | tf_op jit(solution)/shard_map/ppermute | solution.py:52
  33.8 2.9 %collective-permute-start.9 = (bf16[192,588]{1,0:T(8,128)(2,1)S(1)}, bf16[192,588]{1,0:T(8,128)(2,1)S(1)}, u32[]{:S(2)}, u32[]{:S(2)}) collective-permute-start(bf16[192,588]{1,0:T(8,128)(2,1)S(1)} %constant_dynamic-slice_fusion.8.w0), channel_id=1, source_target_pairs={{0,128},{4,132},{8,136},{12,140},{16,144},{20,148},{24,152},{28,15... | collective-permute-start | bytes 677384 | tf_op jit(solution)/shard_map/ppermute | solution.py:56
  38.3 2.5 %collective-permute-start.22 = (bf16[2,96,384]{2,1,0:T(8,128)(2,1)S(1)}, bf16[2,96,384]{2,1,0:T(8,128)(2,1)S(1)}, u32[]{:S(2)}, u32[]{:S(2)}) collective-permute-start(bf16[2,96,384]{2,1,0:T(8,128)(2,1)S(1)} %get-tuple-element.38), channel_id=1, source_target_pairs={{0,8},{4,12},{8,16},{12,20},{16,24},{20,28},{24,32},{28,36},{32,40... | collective-permute-start | bytes 442376 | tf_op jit(solution)/shard_map/ppermute | solution.py:52
  41.8 10.7 %collective-permute-start.30 = (bf16[2,96,384]{2,1,0:T(8,128)(2,1)S(1)}, bf16[2,96,384]{2,1,0:T(8,128)(2,1)S(1)}, u32[]{:S(2)}, u32[]{:S(2)}) collective-permute-start(bf16[2,96,384]{2,1,0:T(8,128)(2,1)S(1)} %get-tuple-element.37), channel_id=1, source_target_pairs={{0,192},{4,196},{8,200},{12,204},{16,208},{20,212},{24,216},{28,22... | collective-permute-start | bytes 442376 | tf_op jit(solution)/shard_map/ppermute | solution.py:56
  52.8 7.0 %collective-permute-start.31 = (bf16[2,96,384]{2,1,0:T(8,128)(2,1)S(1)}, bf16[2,96,384]{2,1,0:T(8,128)(2,1)S(1)}, u32[]{:S(2)}, u32[]{:S(2)}) collective-permute-start(bf16[2,96,384]{2,1,0:T(8,128)(2,1)S(1)} %get-tuple-element.37), channel_id=1, source_target_pairs={{0,128},{4,132},{8,136},{12,140},{16,144},{20,148},{24,152},{28,15... | collective-permute-start | bytes 442376 | tf_op jit(solution)/shard_map/ppermute | solution.py:56
  61.0 3.4 %collective-permute-start.43 = (bf16[48,384]{1,0:T(8,128)(2,1)S(1)}, bf16[48,384]{1,0:T(8,128)(2,1)S(1)}, u32[]{:S(2)}, u32[]{:S(2)}) collective-permute-start(bf16[48,384]{1,0:T(8,128)(2,1)S(1)} %get-tuple-element.28), channel_id=1, source_target_pairs={{0,240},{4,244},{8,248},{12,252},{16,0},{20,4},{24,8},{28,12},{32,... | collective-permute-start | bytes 110600 | tf_op jit(solution)/shard_map/ppermute | solution.py:64
  66.5 3.1 %collective-permute-start.42 = (bf16[4,48,384]{2,1,0:T(8,128)(2,1)S(1)}, bf16[4,48,384]{2,1,0:T(8,128)(2,1)S(1)}, u32[]{:S(2)}, u32[]{:S(2)}) collective-permute-start(bf16[4,48,384]{2,1,0:T(8,128)(2,1)S(1)} %pad_maximum_fusion.2), channel_id=1, source_target_pairs={{0,248},{4,252},{8,0},{12,4},{16,8},{20,12},{24,16},{28,20},{32,24... | collective-permute-start | bytes 442376 | tf_op jit(solution)/shard_map/ppermute | solution.py:64
  69.8 3.0 %collective-permute-start.21 = (bf16[2,96,384]{2,1,0:T(8,128)(2,1)S(1)}, bf16[2,96,384]{2,1,0:T(8,128)(2,1)S(1)}, u32[]{:S(2)}, u32[]{:S(2)}) collective-permute-start(bf16[2,96,384]{2,1,0:T(8,128)(2,1)S(1)} %collective-permute-done.20), channel_id=1, source_target_pairs={{0,56},{4,60},{8,0},{12,4},{16,8},{20,12},{24,16},{28,20},{32,24},... | collective-permute-start | bytes 442376 | tf_op jit(solution)/shard_map/ppermute | solution.py:52
  72.8 2.9 %collective-permute-done.24 = bf16[2,96,384]{2,1,0:T(8,128)(2,1)S(1)} collective-permute-done((bf16[2,96,384]{2,1,0:T(8,128)(2,1)S(1)}, bf16[2,96,384]{2,1,0:T(8,128)(2,1)S(1)}, u32[]{:S(2)}, u32[]{:S(2)}) %collective-permute-start.24) | collective-permute-done | bytes 147488 | tf_op jit(solution)/shard_map/ppermute | solution.py:52
  76.5 5.5 %collective-permute-done.25 = bf16[2,96,384]{2,1,0:T(8,128)(2,1)S(1)} collective-permute-done((bf16[2,96,384]{2,1,0:T(8,128)(2,1)S(1)}, bf16[2,96,384]{2,1,0:T(8,128)(2,1)S(1)}, u32[]{:S(2)}, u32[]{:S(2)}) %collective-permute-start.25) | collective-permute-done | bytes 147488 | tf_op jit(solution)/shard_map/ppermute | solution.py:52
  83.2 3.2 %collective-permute-start.34 = (bf16[8,96,384]{2,1,0:T(8,128)(2,1)}, bf16[8,96,384]{2,1,0:T(8,128)(2,1)}, u32[]{:S(2)}, u32[]{:S(2)}) collective-permute-start(bf16[8,96,384]{2,1,0:T(8,128)(2,1)} %constant_dynamic-slice_fusion.2.refs_15_), channel_id=1, source_target_pairs={{0,56},{4,60},{8,0},{12,4},{16,8},{20,12},{24,16},{28,20},{32,24},... | collective-permute-start | bytes 1769480 | tf_op jit(solution)/shard_map/ppermute | solution.py:52
  90.5 6.0 %collective-permute-done.34.refs_17_ = bf16[8,96,384]{2,1,0:T(8,128)(2,1)} collective-permute-done((bf16[8,96,384]{2,1,0:T(8,128)(2,1)}, bf16[8,96,384]{2,1,0:T(8,128)(2,1)}, u32[]{:S(2)}, u32[]{:S(2)}) %collective-permute-start.34) | collective-permute-done | bytes 589856 | tf_op jit(solution)/shard_map/ppermute | solution.py:52
  96.5 2.7 %collective-permute-start.36 = (bf16[8,96,384]{2,1,0:T(8,128)(2,1)}, bf16[8,96,384]{2,1,0:T(8,128)(2,1)}, u32[]{:S(2)}, u32[]{:S(2)}) collective-permute-start(bf16[8,96,384]{2,1,0:T(8,128)(2,1)} %collective-permute-done.34.refs_17_), channel_id=1, source_target_pairs={{0,56},{4,60},{8,0},{12,4},{16,8},{20,12},{24,16},{28,20},{32,24},... | collective-permute-start | bytes 1769480 | tf_op jit(solution)/shard_map/ppermute | solution.py:52
  117.0 2.8 %collective-permute-start.12 = (bf16[304,768]{1,0:T(8,128)(2,1)S(1)}, bf16[304,768]{1,0:T(8,128)(2,1)S(1)}, u32[]{:S(2)}, u32[]{:S(2)}) collective-permute-start(bf16[304,768]{1,0:T(8,128)(2,1)S(1)} %embed.1.refs_2_.e_own), channel_id=1, source_target_pairs={{0,2},{1,3},{2,0},{3,1},{4,6},{5,7},{6,4},{7,5},{8,10},{9,11},{10,... | collective-permute-start | bytes 1400840 | tf_op jit(solution)/shard_map/ppermute | solution.py:60
  124.6 2.6 %collective-permute-done.12.refs_4_ = bf16[304,768]{1,0:T(8,128)(2,1)S(1)} collective-permute-done((bf16[304,768]{1,0:T(8,128)(2,1)S(1)}, bf16[304,768]{1,0:T(8,128)(2,1)S(1)}, u32[]{:S(2)}, u32[]{:S(2)}) %collective-permute-start.12) | collective-permute-done | bytes 466976 | tf_op jit(solution)/shard_map/ppermute | solution.py:60
  128.8 6.6 %collective-permute-done.11.refs_3_ = bf16[304,768]{1,0:T(8,128)(2,1)S(1)} collective-permute-done((bf16[304,768]{1,0:T(8,128)(2,1)S(1)}, bf16[304,768]{1,0:T(8,128)(2,1)S(1)}, u32[]{:S(2)}, u32[]{:S(2)}) %collective-permute-start.11) | collective-permute-done | bytes 466976 | tf_op jit(solution)/shard_map/ppermute | solution.py:60
  137.6 3.4 %collective-permute-start.40 = (bf16[4,96,384]{2,1,0:T(8,128)(2,1)S(1)}, bf16[4,96,384]{2,1,0:T(8,128)(2,1)S(1)}, u32[]{:S(2)}, u32[]{:S(2)}) collective-permute-start(bf16[4,96,384]{2,1,0:T(8,128)(2,1)S(1)} %slice.312), channel_id=1, source_target_pairs={{0,56},{4,60},{8,0},{12,4},{16,8},{20,12},{24,16},{28,20},{32,24},... | collective-permute-start | bytes 884744 | tf_op jit(solution)/shard_map/ppermute | solution.py:52
  141.5 9.7 %collective-permute-done.29.refs_14_ = bf16[768,384]{1,0:T(8,128)(2,1)S(1)} collective-permute-done((bf16[768,384]{1,0:T(8,128)(2,1)S(1)}, bf16[768,384]{1,0:T(8,128)(2,1)S(1)}, u32[]{:S(2)}, u32[]{:S(2)}) %collective-permute-start.29) | collective-permute-done | bytes 589856 | tf_op jit(solution)/shard_map/ppermute | solution.py:56
  152.9 22.7 %layer.1 = (bf16[288,384]{1,0:T(8,128)(2,1)S(1)}, bf16[4,288,768]{2,1,0:T(8,128)(2,1)}, bf16[4,288,768]{2,1,0:T(8,128)(2,1)}, f32[16,288]{1,0:T(8,128)S(1)}, f32[288,128]{1,0:T(8,128)S(1)}) custom-call(s32[4]{0:T(128)S(1)} %pad_add_fusion.place.refs_0_, s32[6]{0:T(128)S(1)} %get-tuple-element.16.refs_1_, bf16[304,768]{1,0:T(8,128)(2,1)S(1)} %embed.1.refs_2_.e_own, ...), custom_call_target="tpu_custom_call" | custom-call | flops 5435817984 | bytes 20000000 | tf_op jit(solution)/shard_map/layer/pallas_call | solution.py:295
  181.3 2.7 %collective-permute-start.50 = (bf16[288,768]{1,0:T(8,128)(2,1)S(1)}, bf16[288,768]{1,0:T(8,128)(2,1)S(1)}, u32[]{:S(2)}, u32[]{:S(2)}) collective-permute-start(bf16[288,768]{1,0:T(8,128)(2,1)S(1)} %get-tuple-element.20), channel_id=1, source_target_pairs={{0,3},{1,0},{2,1},{3,2},{4,7},{5,4},{6,5},{7,6},{8,11},{9,8},{10,9... | collective-permute-start | bytes 1327112 | tf_op jit(solution)/shard_map/ppermute | solution.py:60
  185.8 3.3 %collective-permute-start.54 = (f32[16,288]{1,0:T(8,128)S(1)}, f32[16,288]{1,0:T(8,128)S(1)}, u32[]{:S(2)}, u32[]{:S(2)}) collective-permute-start(f32[16,288]{1,0:T(8,128)S(1)} %add.186.s0), channel_id=1, source_target_pairs={{0,3},{1,0},{2,1},{3,2},{4,7},{5,4},{6,5},{7,6},{8,11},{9,8},{10,9... | collective-permute-start | bytes 55304 | tf_op jit(solution)/shard_map/ppermute | solution.py:60
  189.8 14.6 %collective-permute-done.54.s3 = f32[16,288]{1,0:T(8,128)S(1)} collective-permute-done((f32[16,288]{1,0:T(8,128)S(1)}, f32[16,288]{1,0:T(8,128)S(1)}, u32[]{:S(2)}, u32[]{:S(2)}) %collective-permute-start.54) | collective-permute-done | bytes 18464 | tf_op jit(solution)/shard_map/ppermute | solution.py:60
  207.5 4.4 %collective-permute-start.45 = (bf16[48,384]{1,0:T(8,128)(2,1)S(1)}, bf16[48,384]{1,0:T(8,128)(2,1)S(1)}, u32[]{:S(2)}, u32[]{:S(2)}) collective-permute-start(bf16[48,384]{1,0:T(8,128)(2,1)S(1)} %get-tuple-element.51), channel_id=1, source_target_pairs={{0,16},{4,20},{8,24},{12,28},{16,32},{20,36},{24,40},{28,44},{32,4... | collective-permute-start | bytes 110600 | tf_op jit(solution)/shard_map/ppermute | solution.py:64
  214.9 3.2 %collective-permute-start.57 = (bf16[192,588]{1,0:T(8,128)(2,1)S(1)}, bf16[192,588]{1,0:T(8,128)(2,1)S(1)}, u32[]{:S(2)}, u32[]{:S(2)}) collective-permute-start(bf16[192,588]{1,0:T(8,128)(2,1)S(1)} %get-tuple-element.24), channel_id=1, source_target_pairs={{0,192},{4,196},{8,200},{12,204},{16,208},{20,212},{24,216},{28,22... | collective-permute-start | bytes 677384 | tf_op jit(solution)/shard_map/ppermute | solution.py:56
  218.2 9.2 %collective-permute-done.55 = bf16[192,588]{1,0:T(8,128)(2,1)S(1)} collective-permute-done((bf16[192,588]{1,0:T(8,128)(2,1)S(1)}, bf16[192,588]{1,0:T(8,128)(2,1)S(1)}, u32[]{:S(2)}, u32[]{:S(2)}) %collective-permute-start.55) | collective-permute-done | bytes 225824 | tf_op jit(solution)/shard_map/ppermute | solution.py:56
  227.7 2.7 %collective-permute-start.58 = (bf16[24,588]{1,0:T(8,128)(2,1)S(1)}, bf16[24,588]{1,0:T(8,128)(2,1)S(1)}, u32[]{:S(2)}, u32[]{:S(2)}) collective-permute-start(bf16[24,588]{1,0:T(8,128)(2,1)S(1)} %get-tuple-element.41), channel_id=1, source_target_pairs={{0,8},{4,12},{8,16},{12,20},{16,24},{20,28},{24,32},{28,36},{32,40... | collective-permute-start | bytes 84680 | tf_op jit(solution)/shard_map/ppermute | solution.py:52
  231.7 2.6 %collective-permute-start.63 = (bf16[24,588]{1,0:T(8,128)(2,1)S(1)}, bf16[24,588]{1,0:T(8,128)(2,1)S(1)}, u32[]{:S(2)}, u32[]{:S(2)}) collective-permute-start(bf16[24,588]{1,0:T(8,128)(2,1)S(1)} %get-tuple-element.43), channel_id=1, source_target_pairs={{0,48},{4,52},{8,56},{12,60},{16,0},{20,4},{24,8},{28,12},{32,16},... | collective-permute-start | bytes 84680 | tf_op jit(solution)/shard_map/ppermute | solution.py:52
  236.4 4.4 %collective-permute-start.61 = (bf16[24,588]{1,0:T(8,128)(2,1)S(1)}, bf16[24,588]{1,0:T(8,128)(2,1)S(1)}, u32[]{:S(2)}, u32[]{:S(2)}) collective-permute-start(bf16[24,588]{1,0:T(8,128)(2,1)S(1)} %get-tuple-element.45), channel_id=1, source_target_pairs={{0,32},{4,36},{8,40},{12,44},{16,48},{20,52},{24,56},{28,60},{32,0... | collective-permute-start | bytes 84680 | tf_op jit(solution)/shard_map/ppermute | solution.py:52
  244.2 3.8 %collective-permute-done.60 = bf16[24,588]{1,0:T(8,128)(2,1)S(1)} collective-permute-done((bf16[24,588]{1,0:T(8,128)(2,1)S(1)}, bf16[24,588]{1,0:T(8,128)(2,1)S(1)}, u32[]{:S(2)}, u32[]{:S(2)}) %collective-permute-start.60) | collective-permute-done | bytes 28256 | tf_op jit(solution)/shard_map/ppermute | solution.py:52
  (214 shorter events, 64.8 us)
Async XLA Ops:
  0.6 31.3 %collective-permute-start.7 = (bf16[24,588]{1,0:T(8,128)(2,1)}, bf16[24,588]{1,0:T(8,128)(2,1)S(1)}, u32[]{:S(2)}, u32[]{:S(2)}) collective-permute-start(bf16[24,588]{1,0:T(8,128)(2,1)} %bitcast.257), channel_id=1, source_target_pairs={{0,8},{4,12},{8,16},{12,20},{16,24},{20,28},{24,32},{28,36},{32,40... | collective-permute-start | bytes 84680 | tf_op jit(solution)/shard_map/ppermute | solution.py:52
  2.6 29.3 %collective-permute-start.6 = (bf16[24,588]{1,0:T(8,128)(2,1)}, bf16[24,588]{1,0:T(8,128)(2,1)S(1)}, u32[]{:S(2)}, u32[]{:S(2)}) collective-permute-start(bf16[24,588]{1,0:T(8,128)(2,1)} %bitcast.258), channel_id=1, source_target_pairs={{0,16},{4,20},{8,24},{12,28},{16,32},{20,36},{24,40},{28,44},{32,4... | collective-permute-start | bytes 84680 | tf_op jit(solution)/shard_map/ppermute | solution.py:52
  7.1 24.7 %collective-permute-start.5 = (bf16[24,588]{1,0:T(8,128)(2,1)}, bf16[24,588]{1,0:T(8,128)(2,1)S(1)}, u32[]{:S(2)}, u32[]{:S(2)}) collective-permute-start(bf16[24,588]{1,0:T(8,128)(2,1)} %bitcast.259), channel_id=1, source_target_pairs={{0,24},{4,28},{8,32},{12,36},{16,40},{20,44},{24,48},{28,52},{32,5... | collective-permute-start | bytes 84680 | tf_op jit(solution)/shard_map/ppermute | solution.py:52
  9.0 22.2 %collective-permute-start.4 = (bf16[24,588]{1,0:T(8,128)(2,1)}, bf16[24,588]{1,0:T(8,128)(2,1)S(1)}, u32[]{:S(2)}, u32[]{:S(2)}) collective-permute-start(bf16[24,588]{1,0:T(8,128)(2,1)} %bitcast.260), channel_id=1, source_target_pairs={{0,32},{4,36},{8,40},{12,44},{16,48},{20,52},{24,56},{28,60},{32,0... | collective-permute-start | bytes 84680 | tf_op jit(solution)/shard_map/ppermute | solution.py:52
  33.8 18.9 %collective-permute-start.9 = (bf16[192,588]{1,0:T(8,128)(2,1)S(1)}, bf16[192,588]{1,0:T(8,128)(2,1)S(1)}, u32[]{:S(2)}, u32[]{:S(2)}) collective-permute-start(bf16[192,588]{1,0:T(8,128)(2,1)S(1)} %constant_dynamic-slice_fusion.8.w0), channel_id=1, source_target_pairs={{0,128},{4,132},{8,136},{12,140},{16,144},{20,148},{24,152},{28,15... | collective-permute-start | bytes 677384 | tf_op jit(solution)/shard_map/ppermute | solution.py:56
  36.7 16.1 %collective-permute-start.8 = (bf16[192,588]{1,0:T(8,128)(2,1)S(1)}, bf16[192,588]{1,0:T(8,128)(2,1)S(1)}, u32[]{:S(2)}, u32[]{:S(2)}) collective-permute-start(bf16[192,588]{1,0:T(8,128)(2,1)S(1)} %constant_dynamic-slice_fusion.8.w0), channel_id=1, source_target_pairs={{0,192},{4,196},{8,200},{12,204},{16,208},{20,212},{24,216},{28,22... | collective-permute-start | bytes 677384 | tf_op jit(solution)/shard_map/ppermute | solution.py:56
  38.3 22.7 %collective-permute-start.22 = (bf16[2,96,384]{2,1,0:T(8,128)(2,1)S(1)}, bf16[2,96,384]{2,1,0:T(8,128)(2,1)S(1)}, u32[]{:S(2)}, u32[]{:S(2)}) collective-permute-start(bf16[2,96,384]{2,1,0:T(8,128)(2,1)S(1)} %get-tuple-element.38), channel_id=1, source_target_pairs={{0,8},{4,12},{8,16},{12,20},{16,24},{20,28},{24,32},{28,36},{32,40... | collective-permute-start | bytes 442376 | tf_op jit(solution)/shard_map/ppermute | solution.py:52
  40.9 23.5 %collective-permute-start.19 = (bf16[2,96,384]{2,1,0:T(8,128)(2,1)S(1)}, bf16[2,96,384]{2,1,0:T(8,128)(2,1)S(1)}, u32[]{:S(2)}, u32[]{:S(2)}) collective-permute-start(bf16[2,96,384]{2,1,0:T(8,128)(2,1)S(1)} %get-tuple-element.38), channel_id=1, source_target_pairs={{0,56},{4,60},{8,0},{12,4},{16,8},{20,12},{24,16},{28,20},{32,24},... | collective-permute-start | bytes 442376 | tf_op jit(solution)/shard_map/ppermute | solution.py:52
  41.8 22.6 %collective-permute-start.30 = (bf16[2,96,384]{2,1,0:T(8,128)(2,1)S(1)}, bf16[2,96,384]{2,1,0:T(8,128)(2,1)S(1)}, u32[]{:S(2)}, u32[]{:S(2)}) collective-permute-start(bf16[2,96,384]{2,1,0:T(8,128)(2,1)S(1)} %get-tuple-element.37), channel_id=1, source_target_pairs={{0,192},{4,196},{8,200},{12,204},{16,208},{20,212},{24,216},{28,22... | collective-permute-start | bytes 442376 | tf_op jit(solution)/shard_map/ppermute | solution.py:56
  52.7 17.0 %collective-permute-start.32 = (bf16[2,96,384]{2,1,0:T(8,128)(2,1)S(1)}, bf16[2,96,384]{2,1,0:T(8,128)(2,1)S(1)}, u32[]{:S(2)}, u32[]{:S(2)}) collective-permute-start(bf16[2,96,384]{2,1,0:T(8,128)(2,1)S(1)} %get-tuple-element.37), channel_id=1, source_target_pairs={{0,64},{4,68},{8,72},{12,76},{16,80},{20,84},{24,88},{28,92},{32,9... | collective-permute-start | bytes 442376 | tf_op jit(solution)/shard_map/ppermute | solution.py:56
  52.8 13.8 %collective-permute-start.31 = (bf16[2,96,384]{2,1,0:T(8,128)(2,1)S(1)}, bf16[2,96,384]{2,1,0:T(8,128)(2,1)S(1)}, u32[]{:S(2)}, u32[]{:S(2)}) collective-permute-start(bf16[2,96,384]{2,1,0:T(8,128)(2,1)S(1)} %get-tuple-element.37), channel_id=1, source_target_pairs={{0,128},{4,132},{8,136},{12,140},{16,144},{20,148},{24,152},{28,15... | collective-permute-start | bytes 442376 | tf_op jit(solution)/shard_map/ppermute | solution.py:56
  61.0 25.8 %collective-permute-start.43 = (bf16[48,384]{1,0:T(8,128)(2,1)S(1)}, bf16[48,384]{1,0:T(8,128)(2,1)S(1)}, u32[]{:S(2)}, u32[]{:S(2)}) collective-permute-start(bf16[48,384]{1,0:T(8,128)(2,1)S(1)} %get-tuple-element.28), channel_id=1, source_target_pairs={{0,240},{4,244},{8,248},{12,252},{16,0},{20,4},{24,8},{28,12},{32,... | collective-permute-start | bytes 110600 | tf_op jit(solution)/shard_map/ppermute | solution.py:64
  66.5 21.1 %collective-permute-start.42 = (bf16[4,48,384]{2,1,0:T(8,128)(2,1)S(1)}, bf16[4,48,384]{2,1,0:T(8,128)(2,1)S(1)}, u32[]{:S(2)}, u32[]{:S(2)}) collective-permute-start(bf16[4,48,384]{2,1,0:T(8,128)(2,1)S(1)} %pad_maximum_fusion.2), channel_id=1, source_target_pairs={{0,248},{4,252},{8,0},{12,4},{16,8},{20,12},{24,16},{28,20},{32,24... | collective-permute-start | bytes 442376 | tf_op jit(solution)/shard_map/ppermute | solution.py:64
  69.7 29.8 %collective-permute-start.14 = (bf16[304,768]{1,0:T(8,128)(2,1)S(1)}, bf16[304,768]{1,0:T(8,128)(2,1)S(1)}, u32[]{:S(2)}, u32[]{:S(2)}) collective-permute-start(bf16[304,768]{1,0:T(8,128)(2,1)S(1)} %embed.1.refs_2_.e_own), channel_id=1, source_target_pairs={{0,4},{4,0},{8,12},{12,8},{16,20},{20,16},{24,28},{28,24},{32,36},... | collective-permute-start | bytes 1400840 | tf_op jit(solution)/shard_map/ppermute | solution.py:48
  86.8 35.1 %collective-permute-start.27 = (bf16[2,768,384]{2,1,0:T(8,128)(2,1)S(1)}, bf16[2,768,384]{2,1,0:T(8,128)(2,1)}, u32[]{:S(2)}, u32[]{:S(2)}) collective-permute-start(bf16[2,768,384]{2,1,0:T(8,128)(2,1)S(1)} %constant_dynamic-slice_fusion.3.refs_10_), channel_id=1, source_target_pairs={{0,192},{4,196},{8,200},{12,204},{16,208},{20,212},{24,216},{28,22... | collective-permute-start | bytes 3538952 | tf_op jit(solution)/shard_map/ppermute | solution.py:56
  87.7 39.5 %collective-permute-start.26 = (bf16[2,768,384]{2,1,0:T(8,128)(2,1)S(1)}, bf16[2,768,384]{2,1,0:T(8,128)(2,1)}, u32[]{:S(2)}, u32[]{:S(2)}) collective-permute-start(bf16[2,768,384]{2,1,0:T(8,128)(2,1)S(1)} %constant_dynamic-slice_fusion.3.refs_10_), channel_id=1, source_target_pairs={{0,64},{4,68},{8,72},{12,76},{16,80},{20,84},{24,88},{28,92},{32,9... | collective-permute-start | bytes 3538952 | tf_op jit(solution)/shard_map/ppermute | solution.py:56
  96.5 23.3 %collective-permute-start.36 = (bf16[8,96,384]{2,1,0:T(8,128)(2,1)}, bf16[8,96,384]{2,1,0:T(8,128)(2,1)}, u32[]{:S(2)}, u32[]{:S(2)}) collective-permute-start(bf16[8,96,384]{2,1,0:T(8,128)(2,1)} %collective-permute-done.34.refs_17_), channel_id=1, source_target_pairs={{0,56},{4,60},{8,0},{12,4},{16,8},{20,12},{24,16},{28,20},{32,24},... | collective-permute-start | bytes 1769480 | tf_op jit(solution)/shard_map/ppermute | solution.py:52
  99.2 22.7 %collective-permute-start.35 = (bf16[8,96,384]{2,1,0:T(8,128)(2,1)}, bf16[8,96,384]{2,1,0:T(8,128)(2,1)}, u32[]{:S(2)}, u32[]{:S(2)}) collective-permute-start(bf16[8,96,384]{2,1,0:T(8,128)(2,1)} %collective-permute-done.33.refs_16_), channel_id=1, source_target_pairs={{0,8},{4,12},{8,16},{12,20},{16,24},{20,28},{24,32},{28,36},{32,40... | collective-permute-start | bytes 1769480 | tf_op jit(solution)/shard_map/ppermute | solution.py:52
  99.4 17.5 %collective-permute-start.13 = (bf16[304,768]{1,0:T(8,128)(2,1)S(1)}, bf16[304,768]{1,0:T(8,128)(2,1)S(1)}, u32[]{:S(2)}, u32[]{:S(2)}) collective-permute-start(bf16[304,768]{1,0:T(8,128)(2,1)S(1)} %embed.1.refs_2_.e_own), channel_id=1, source_target_pairs={{0,1},{1,2},{2,3},{3,0},{4,5},{5,6},{6,7},{7,4},{8,9},{9,10},{10,1... | collective-permute-start | bytes 1400840 | tf_op jit(solution)/shard_map/ppermute | solution.py:60
  119.8 15.6 %collective-permute-start.38 = (bf16[8,96,384]{2,1,0:T(8,128)(2,1)}, bf16[8,96,384]{2,1,0:T(8,128)(2,1)S(1)}, u32[]{:S(2)}, u32[]{:S(2)}) collective-permute-start(bf16[8,96,384]{2,1,0:T(8,128)(2,1)} %collective-permute-done.36.refs_19_), channel_id=1, source_target_pairs={{0,56},{4,60},{8,0},{12,4},{16,8},{20,12},{24,16},{28,20},{32,24},... | collective-permute-start | bytes 1769480 | tf_op jit(solution)/shard_map/ppermute | solution.py:52
  121.9 14.4 %collective-permute-start.37 = (bf16[8,96,384]{2,1,0:T(8,128)(2,1)}, bf16[8,96,384]{2,1,0:T(8,128)(2,1)S(1)}, u32[]{:S(2)}, u32[]{:S(2)}) collective-permute-start(bf16[8,96,384]{2,1,0:T(8,128)(2,1)} %collective-permute-done.35.refs_18_), channel_id=1, source_target_pairs={{0,8},{4,12},{8,16},{12,20},{16,24},{20,28},{24,32},{28,36},{32,40... | collective-permute-start | bytes 1769480 | tf_op jit(solution)/shard_map/ppermute | solution.py:52
  121.9 13.5 %collective-permute-start.11 = (bf16[304,768]{1,0:T(8,128)(2,1)S(1)}, bf16[304,768]{1,0:T(8,128)(2,1)S(1)}, u32[]{:S(2)}, u32[]{:S(2)}) collective-permute-start(bf16[304,768]{1,0:T(8,128)(2,1)S(1)} %embed.1.refs_2_.e_own), channel_id=1, source_target_pairs={{0,3},{1,0},{2,1},{3,2},{4,7},{5,4},{6,5},{7,6},{8,11},{9,8},{10,9... | collective-permute-start | bytes 1400840 | tf_op jit(solution)/shard_map/ppermute | solution.py:60
  127.1 13.9 %collective-permute-start.16 = (bf16[304,768]{1,0:T(8,128)(2,1)S(1)}, bf16[304,768]{1,0:T(8,128)(2,1)S(1)}, u32[]{:S(2)}, u32[]{:S(2)}) collective-permute-start(bf16[304,768]{1,0:T(8,128)(2,1)S(1)} %collective-permute-done.12.refs_4_), channel_id=1, source_target_pairs={{0,4},{4,0},{8,12},{12,8},{16,20},{20,16},{24,28},{28,24},{32,36},... | collective-permute-start | bytes 1400840 | tf_op jit(solution)/shard_map/ppermute | solution.py:48
  135.4 15.8 %collective-permute-start.29 = (bf16[768,384]{1,0:T(8,128)(2,1)S(1)}, bf16[768,384]{1,0:T(8,128)(2,1)S(1)}, u32[]{:S(2)}, u32[]{:S(2)}) collective-permute-start(bf16[768,384]{1,0:T(8,128)(2,1)S(1)} %slice_bitcast_fusion), channel_id=1, source_target_pairs={{0,192},{4,196},{8,200},{12,204},{16,208},{20,212},{24,216},{28,22... | collective-permute-start | bytes 1769480 | tf_op jit(solution)/shard_map/ppermute | solution.py:56
  136.3 16.6 %collective-permute-start.28 = (bf16[768,384]{1,0:T(8,128)(2,1)S(1)}, bf16[768,384]{1,0:T(8,128)(2,1)S(1)}, u32[]{:S(2)}, u32[]{:S(2)}) collective-permute-start(bf16[768,384]{1,0:T(8,128)(2,1)S(1)} %slice_bitcast_fusion.1), channel_id=1, source_target_pairs={{0,64},{4,68},{8,72},{12,76},{16,80},{20,84},{24,88},{28,92},{32,9... | collective-permute-start | bytes 1769480 | tf_op jit(solution)/shard_map/ppermute | solution.py:56
  137.6 15.2 %collective-permute-start.40 = (bf16[4,96,384]{2,1,0:T(8,128)(2,1)S(1)}, bf16[4,96,384]{2,1,0:T(8,128)(2,1)S(1)}, u32[]{:S(2)}, u32[]{:S(2)}) collective-permute-start(bf16[4,96,384]{2,1,0:T(8,128)(2,1)S(1)} %slice.312), channel_id=1, source_target_pairs={{0,56},{4,60},{8,0},{12,4},{16,8},{20,12},{24,16},{28,20},{32,24},... | collective-permute-start | bytes 884744 | tf_op jit(solution)/shard_map/ppermute | solution.py:52
  181.3 30.9 %collective-permute-start.50 = (bf16[288,768]{1,0:T(8,128)(2,1)S(1)}, bf16[288,768]{1,0:T(8,128)(2,1)S(1)}, u32[]{:S(2)}, u32[]{:S(2)}) collective-permute-start(bf16[288,768]{1,0:T(8,128)(2,1)S(1)} %get-tuple-element.20), channel_id=1, source_target_pairs={{0,3},{1,0},{2,1},{3,2},{4,7},{5,4},{6,5},{7,6},{8,11},{9,8},{10,9... | collective-permute-start | bytes 1327112 | tf_op jit(solution)/shard_map/ppermute | solution.py:60
  184.0 28.2 %collective-permute-start.49 = (bf16[288,768]{1,0:T(8,128)(2,1)S(1)}, bf16[288,768]{1,0:T(8,128)(2,1)S(1)}, u32[]{:S(2)}, u32[]{:S(2)}) collective-permute-start(bf16[288,768]{1,0:T(8,128)(2,1)S(1)} %get-tuple-element.21), channel_id=1, source_target_pairs={{0,2},{1,3},{2,0},{3,1},{4,6},{5,7},{6,4},{7,5},{8,10},{9,11},{10,... | collective-permute-start | bytes 1327112 | tf_op jit(solution)/shard_map/ppermute | solution.py:60
  185.7 26.5 %collective-permute-start.48 = (bf16[288,768]{1,0:T(8,128)(2,1)S(1)}, bf16[288,768]{1,0:T(8,128)(2,1)S(1)}, u32[]{:S(2)}, u32[]{:S(2)}) collective-permute-start(bf16[288,768]{1,0:T(8,128)(2,1)S(1)} %get-tuple-element.22), channel_id=1, source_target_pairs={{0,1},{1,2},{2,3},{3,0},{4,5},{5,6},{6,7},{7,4},{8,9},{9,10},{10,1... | collective-permute-start | bytes 1327112 | tf_op jit(solution)/shard_map/ppermute | solution.py:60
  185.8 18.6 %collective-permute-start.54 = (f32[16,288]{1,0:T(8,128)S(1)}, f32[16,288]{1,0:T(8,128)S(1)}, u32[]{:S(2)}, u32[]{:S(2)}) collective-permute-start(f32[16,288]{1,0:T(8,128)S(1)} %add.186.s0), channel_id=1, source_target_pairs={{0,3},{1,0},{2,1},{3,2},{4,7},{5,4},{6,5},{7,6},{8,11},{9,8},{10,9... | collective-permute-start | bytes 55304 | tf_op jit(solution)/shard_map/ppermute | solution.py:60
  189.1 18.4 %collective-permute-start.53 = (f32[16,288]{1,0:T(8,128)S(1)}, f32[16,288]{1,0:T(8,128)S(1)}, u32[]{:S(2)}, u32[]{:S(2)}) collective-permute-start(f32[16,288]{1,0:T(8,128)S(1)} %add.186.s0), channel_id=1, source_target_pairs={{0,2},{1,3},{2,0},{3,1},{4,6},{5,7},{6,4},{7,5},{8,10},{9,11},{10,... | collective-permute-start | bytes 55304 | tf_op jit(solution)/shard_map/ppermute | solution.py:60
  218.1 18.3 %collective-permute-start.46 = (bf16[192,384]{1,0:T(8,128)(2,1)S(1)}, bf16[192,384]{1,0:T(8,128)(2,1)S(1)}, u32[]{:S(2)}, u32[]{:S(2)}) collective-permute-start(bf16[192,384]{1,0:T(8,128)(2,1)S(1)} %get-tuple-element.27), channel_id=1, source_target_pairs={{0,4},{4,0},{8,12},{12,8},{16,20},{20,16},{24,28},{28,24},{32,36},... | collective-permute-start | bytes 442376 | tf_op jit(solution)/shard_map/ppermute | solution.py:48
  (39 other events, 464.3 us)
